TPU v7x, 512 devices: a whole 4x8x8 slice. The times are simulated.
512 devices in a mesh: gx: 8 (over y), gy: 8 (over z), gz: 8 (over x, core).
Axes of the slice: x: 4, y: 8, z: 8, core: 2. Of those that a mesh axis runs over, the one named last changes fastest.
Arguments:
- point_offset: float32 [3, 8, 8, 8, 128, 128], P(None, 'gx', 'gy', 'gz'), may hold values from 0 to 1
- point_mass: float32 [8, 8, 8, 128, 128], P('gx', 'gy', 'gz'), may hold values from 0.3 to 3
- point_velocity: float32 [3, 8, 8, 8, 128, 128], P(None, 'gx', 'gy', 'gz'), may hold values from -6 to 6
- point_stiffness: float32 [8, 8, 8, 128, 128], P('gx', 'gy', 'gz'), may hold values from 0.1 to 2
- cell_index: int32 [8, 8, 8, 128], P('gx', 'gy', 'gz'), may hold values from 0 to 8191, as said below
- live_count: int32 [8, 8, 8, 128], P('gx', 'gy', 'gz'), may hold values from 1 to 128
Outputs:
- grid_velocity: float32 [3, 64, 64, 1024], P(None, 'gx', 'gy', 'gz')
- point_update: float32 [3, 8, 8, 8, 128, 128], P(None, 'gx', 'gy', 'gz')
Inputs may be any that keep to these rules, and one draw needn't show every extreme that they name: `cell_index`: every value from 0 to 8191 may occur, several blocks may share a cell.
All inputs are finite; a program needn't handle non-finite values.
Results may differ from a plain program's by a relative error of at most 0.0003.
Values sent between devices are 32-bit elements; how exact they have to be, the bound alone decides.
A program may use at most 64 MiB of HBM per device.

v0:
```python
import jax
import jax.numpy as jnp
from jax import lax
from jax.sharding import PartitionSpec as P

CX = 8
CY = 8
CZ = 128
NB = 128
PTS = 128
NEWTON = 2
CG = 4


HIGH = lax.Precision.HIGHEST
BETA = 0.5
GAMMA = 0.3


def from_behind(block, axis, distance):
    devices = range(lax.axis_size(axis))
    route = [((i - distance) % len(devices), i) for i in devices]
    return lax.ppermute(block, axis, route)


def extended(value, sides, width):
    for axis, dim in sides:
        size, length = (lax.axis_size(axis), value.shape[dim])
        up = [(i, (i + 1) % size) for i in range(size)]
        down = [(j, i) for i, j in up]
        last = lax.slice_in_dim(value, length - width, length, axis=dim)
        first = lax.slice_in_dim(value, 0, width, axis=dim)
        before = lax.ppermute(last, axis, up)
        after = lax.ppermute(first, axis, down)
        value = jnp.concatenate([before, value, after], axis=dim)
    return value


def corner_weights(frac):
    fx, fy, fz = (frac[0], frac[1], frac[2])
    result = []
    for a in range(2):
        for b in range(2):
            for c in range(2):
                wx = fx if a == 1 else 1.0 - fx
                wy = fy if b == 1 else 1.0 - fy
                wz = fz if c == 1 else 1.0 - fz
                result.append(wx * wy * wz)
    return jnp.stack(result)


def offsets():
    found = []
    for dx in (-1, 0, 1):
        for dy in (-1, 0, 1):
            for dz in (-1, 0, 1):
                if dx != 0 or dy != 0 or dz != 0:
                    found.append((dx, dy, dz))
    return found


def fold_z(stacked):
    edge = lax.slice_in_dim(stacked, stacked.shape[5] - 1, stacked.shape[5], axis=5)
    incoming = from_behind(edge, "gz", 1)
    return jnp.concatenate(
        [incoming, lax.slice_in_dim(stacked, 0, stacked.shape[5] - 1, axis=5)], axis=5
    )


def fold_y(stacked):
    edge = lax.slice_in_dim(stacked, stacked.shape[3] - 1, stacked.shape[3], axis=3)
    incoming = from_behind(edge, "gy", 1)
    return jnp.concatenate(
        [incoming, lax.slice_in_dim(stacked, 0, stacked.shape[3] - 1, axis=3)], axis=3
    )


def fold_x(stacked):
    edge = lax.slice_in_dim(stacked, stacked.shape[1] - 1, stacked.shape[1], axis=1)
    incoming = from_behind(edge, "gx", 1)
    return jnp.concatenate(
        [incoming, lax.slice_in_dim(stacked, 0, stacked.shape[1] - 1, axis=1)], axis=1
    )


def extend(field):
    return extended(field, (("gx", 1), ("gy", 2), ("gz", 3)), 1)


def neighbor(padded, dx, dy, dz):
    return padded[:, 1 + dx : 1 + dx + CX, 1 + dy : 1 + dy + CY, 1 + dz : 1 + dz + CZ]


def global_dot(first, second):
    return lax.psum(jnp.sum(first * second), ("gx", "gy", "gz"))


def shards(point_offset, point_mass, point_velocity, point_stiffness, cell_index, live_count):
    cells_dev = CX * CY * CZ
    frac = point_offset.reshape(3, NB, PTS)
    cells = cell_index.reshape(NB)
    mask = (jnp.arange(PTS, dtype=jnp.int32)[None, :] < live_count.reshape(NB)[:, None]).astype(
        jnp.float32
    )
    mass = point_mass.reshape(NB, PTS) * mask
    vel = point_velocity.reshape(3, NB, PTS)
    data = jnp.stack(
        [mass, mass * vel[0], mass * vel[1], mass * vel[2], point_stiffness.reshape(NB, PTS) * mask]
    )
    wts = corner_weights(frac)
    block_sums = jnp.einsum("ebp,kbp->bek", wts, data, precision=HIGH)
    deposits = jax.ops.segment_sum(block_sums.reshape(NB, 40), cells, num_segments=cells_dev)
    deposits = deposits.T.reshape(2, 2, 2, 5, CX, CY, CZ)
    after_z = deposits[:, :, 0] + fold_z(deposits[:, :, 1])
    after_y = after_z[:, 0] + fold_y(after_z[:, 1])
    grid = after_y[0] + fold_x(after_y[1])
    total_mass = grid[0] + 1.0
    target = grid[1:4] / total_mass[None]
    stiff = grid[4] + 0.1
    stiff_pad = extend(stiff[None])
    couplings = []
    for dx, dy, dz in offsets():
        coeff = BETA * 0.5 / float(dx * dx + dy * dy + dz * dz)
        couplings.append((dx, dy, dz, coeff * (stiff + neighbor(stiff_pad, dx, dy, dz)[0])[None]))

    def stencil(field):
        padded = extend(field)
        total = jnp.zeros_like(field)
        for dx, dy, dz, weight in couplings:
            total = total + weight * (field - neighbor(padded, dx, dy, dz))
        return total

    v = target
    for step in range(NEWTON):
        rhs = -(total_mass[None] * (v - target) + GAMMA * total_mass[None] * v * v * v + stencil(v))
        diag = total_mass[None] * (1.0 + 3.0 * GAMMA * v * v)
        x = jnp.zeros_like(v)
        r = rhs
        d = rhs
        rr = global_dot(r, r)
        for it in range(CG):
            image = diag * d + stencil(d)
            alpha = rr / lax.psum(jnp.sum(d * image), ("gx", "gy", "gz"))
            x = x + alpha * d
            r = r - alpha * image
            new_rr = global_dot(r, r)
            d = r + new_rr / rr * d
            rr = new_rr
        v = v + x
    padded = extend(v)
    corner_values = []
    for e in range(8):
        a, b, c = (e // 4, e // 2 % 2, e % 2)
        flat = neighbor(padded, a, b, c).reshape(3, cells_dev)
        corner_values.append(flat[:, cells])
    corner_values = jnp.stack(corner_values)
    out = jnp.einsum("ebp,ekb->kbp", wts, corner_values, precision=HIGH)
    return (v, out.reshape(3, 1, 1, 1, NB, PTS))


def solution(mesh):
    return jax.shard_map(
        shards,
        mesh=mesh,
        in_specs=(
            P(None, "gx", "gy", "gz", None, None),
            P("gx", "gy", "gz", None, None),
            P(None, "gx", "gy", "gz", None, None),
            P("gx", "gy", "gz", None, None),
            P("gx", "gy", "gz", None),
            P("gx", "gy", "gz", None),
        ),
        out_specs=(P(None, "gx", "gy", "gz"), P(None, "gx", "gy", "gz", None, None)),
        check_vma=False,
    )
```

profile of v0, /device:TPU:25, one launch (start us, length us, event | category | flops | bytes accessed | tf_op | source)
XLA Modules:
  0.0 1797.7 jit_solution(7942528451323087705)
XLA Ops:
  28.2 8.0 collective-permute-done.1
  36.4 4.4 collective-permute-start.2
  41.8 4.8 collective-permute-start.3
  54.1 4.6 collective-permute-start.6
  59.5 7.0 collective-permute-start.7
  76.3 5.1 collective-permute-start.11
  118.0 101.1 %all-reduce.1 = (f32[]{:T(128)}, f32[]{:T(128)}) all-reduce(f32[]{:T(128)} %get-tuple-element.17, f32[]{:T(128)} %get-tuple-element.16), channel_id=1, replica_groups=mesh['gx'=8,'gy'=8,'gz'=8] {'gx','gy','gz'}, use_global_device_ids=true, to_apply=%region_2.0 | all-reduce | flops 2 | bytes 16 | tf_op jit(solution)/shard_map/psum | solution.py:95
  221.0 95.3 %psum.114 = f32[]{:T(128)} all-reduce(f32[]{:T(128)} %multiply_reduce_fusion.11), channel_id=1, replica_groups=mesh['gx'=8,'gy'=8,'gz'=8] {'gx','gy','gz'}, use_global_device_ids=true, to_apply=%region_6.0 | all-reduce | flops 1 | bytes 8 | tf_op jit(solution)/shard_map/psum | solution.py:95
  328.7 4.4 collective-permute-start.24
  333.7 4.9 collective-permute-start.25
  345.7 97.1 %psum.115 = f32[]{:T(128)} all-reduce(f32[]{:T(128)} %get-tuple-element.35), channel_id=1, replica_groups=mesh['gx'=8,'gy'=8,'gz'=8] {'gx','gy','gz'}, use_global_device_ids=true, to_apply=%region_8.0 | all-reduce | flops 1 | bytes 8 | tf_op jit(solution)/shard_map/psum | solution.py:143
  444.8 95.6 %psum.116 = f32[]{:T(128)} all-reduce(f32[]{:T(128)} %get-tuple-element.33), channel_id=1, replica_groups=mesh['gx'=8,'gy'=8,'gz'=8] {'gx','gy','gz'}, use_global_device_ids=true, to_apply=%region_10.0 | all-reduce | flops 1 | bytes 8 | tf_op jit(solution)/shard_map/psum | solution.py:95
  557.8 4.9 collective-permute-start.31
  569.8 97.1 %psum.117 = f32[]{:T(128)} all-reduce(f32[]{:T(128)} %get-tuple-element.31), channel_id=1, replica_groups=mesh['gx'=8,'gy'=8,'gz'=8] {'gx','gy','gz'}, use_global_device_ids=true, to_apply=%region_12.0 | all-reduce | flops 1 | bytes 8 | tf_op jit(solution)/shard_map/psum | solution.py:143
  668.9 95.6 %psum.118 = f32[]{:T(128)} all-reduce(f32[]{:T(128)} %multiply_reduce_fusion.7), channel_id=1, replica_groups=mesh['gx'=8,'gy'=8,'gz'=8] {'gx','gy','gz'}, use_global_device_ids=true, to_apply=%region_14.0 | all-reduce | flops 1 | bytes 8 | tf_op jit(solution)/shard_map/psum | solution.py:95
  782.0 4.9 collective-permute-start.37
  794.0 97.1 %psum.119 = f32[]{:T(128)} all-reduce(f32[]{:T(128)} %fusion.291), channel_id=1, replica_groups=mesh['gx'=8,'gy'=8,'gz'=8] {'gx','gy','gz'}, use_global_device_ids=true, to_apply=%region_16.0 | all-reduce | flops 1 | bytes 8 | tf_op jit(solution)/shard_map/psum | solution.py:143
  892.5 4.4 collective-permute-start.39
  904.6 4.6 collective-permute-start.42
  930.5 4.9 collective-permute-start.48
  945.5 99.7 %all-reduce = (f32[]{:T(128)}, f32[]{:T(128)}) all-reduce(f32[]{:T(128)} %get-tuple-element.15, f32[]{:T(128)} %get-tuple-element.14), channel_id=1, replica_groups=mesh['gx'=8,'gy'=8,'gz'=8] {'gx','gy','gz'}, use_global_device_ids=true, to_apply=%region_18.0 | all-reduce | flops 2 | bytes 16 | tf_op jit(solution)/shard_map/psum | solution.py:95
  1047.2 95.5 %psum.122 = f32[]{:T(128)} all-reduce(f32[]{:T(128)} %multiply_reduce_fusion.4), channel_id=1, replica_groups=mesh['gx'=8,'gy'=8,'gz'=8] {'gx','gy','gz'}, use_global_device_ids=true, to_apply=%region_22.0 | all-reduce | flops 1 | bytes 8 | tf_op jit(solution)/shard_map/psum | solution.py:95
  1160.1 4.9 collective-permute-start.55
  1172.0 97.1 %psum.123 = f32[]{:T(128)} all-reduce(f32[]{:T(128)} %get-tuple-element.26), channel_id=1, replica_groups=mesh['gx'=8,'gy'=8,'gz'=8] {'gx','gy','gz'}, use_global_device_ids=true, to_apply=%region_24.0 | all-reduce | flops 1 | bytes 8 | tf_op jit(solution)/shard_map/psum | solution.py:143
  1271.2 95.6 %psum.124 = f32[]{:T(128)} all-reduce(f32[]{:T(128)} %get-tuple-element.24), channel_id=1, replica_groups=mesh['gx'=8,'gy'=8,'gz'=8] {'gx','gy','gz'}, use_global_device_ids=true, to_apply=%region_26.0 | all-reduce | flops 1 | bytes 8 | tf_op jit(solution)/shard_map/psum | solution.py:95
  1384.2 4.9 collective-permute-start.61
  1396.2 97.1 %psum.125 = f32[]{:T(128)} all-reduce(f32[]{:T(128)} %get-tuple-element.22), channel_id=1, replica_groups=mesh['gx'=8,'gy'=8,'gz'=8] {'gx','gy','gz'}, use_global_device_ids=true, to_apply=%region_28.0 | all-reduce | flops 1 | bytes 8 | tf_op jit(solution)/shard_map/psum | solution.py:143
  1495.3 95.6 %psum.126 = f32[]{:T(128)} all-reduce(f32[]{:T(128)} %multiply_reduce_fusion), channel_id=1, replica_groups=mesh['gx'=8,'gy'=8,'gz'=8] {'gx','gy','gz'}, use_global_device_ids=true, to_apply=%region_30.0 | all-reduce | flops 1 | bytes 8 | tf_op jit(solution)/shard_map/psum | solution.py:95
  1608.3 4.9 collective-permute-start.67
  1620.3 97.1 %psum.127 = f32[]{:T(128)} all-reduce(f32[]{:T(128)} %fusion.20), channel_id=1, replica_groups=mesh['gx'=8,'gy'=8,'gz'=8] {'gx','gy','gz'}, use_global_device_ids=true, to_apply=%region_32.0 | all-reduce | flops 1 | bytes 8 | tf_op jit(solution)/shard_map/psum | solution.py:143
  1718.8 4.4 collective-permute-start.69
  1730.9 4.8 collective-permute-start.72
  (293 shorter events, 329.0 us)
Async XLA Ops:
  24.2 12.1 collective-permute-start.1
  41.8 6.8 collective-permute-start.3
  52.2 6.5 collective-permute-start.5
  59.5 12.5 collective-permute-start.7
  68.7 5.7 collective-permute-start.9
  74.3 7.2 collective-permute-start.10
  76.3 6.0 collective-permute-start.11
  82.4 6.8 collective-permute-start.12
  86.0 5.9 collective-permute-start.14
  100.4 7.1 collective-permute-start.17
  326.2 7.0 collective-permute-start.23
  333.7 8.0 collective-permute-start.25
  550.3 6.5 collective-permute-start.29
  557.8 8.0 collective-permute-start.31
  774.5 6.5 collective-permute-start.35
  782.0 8.0 collective-permute-start.37
  892.5 6.4 collective-permute-start.39
  902.6 6.5 collective-permute-start.41
  910.2 7.0 collective-permute-start.43
  914.0 5.9 collective-permute-start.44
  928.4 7.1 collective-permute-start.47
  930.5 5.7 collective-permute-start.48
  938.2 5.9 collective-permute-start.50
  1152.5 6.5 collective-permute-start.53
  1160.1 8.0 collective-permute-start.55
  1376.7 6.5 collective-permute-start.59
  1384.2 8.0 collective-permute-start.61
  1600.8 6.5 collective-permute-start.65
  1608.3 8.0 collective-permute-start.67
  1718.8 6.4 collective-permute-start.69
  1729.0 6.7 collective-permute-start.71
  1736.4 9.8 collective-permute-start.73
  (44 other events, 269.5 us)
where the time goes:
time: 1810 us; the launch traced here: 1800 us
  blocking collectives  1360 us (75%)
  starting transfers between devices  213 us (12%)
  waiting for transfers between devices  108 us (6%)
  local copies, waits for them, and re-layouts  64.3 us (4%)
  other arithmetic  31.4 us (2%)
  between operations  21 us (1%)
    psum x8, blocking collectives, global_dot(): return lax.psum(jnp.sum(first * second), ('gx', 'gy', 'gz'))  774 us
    psum x6, blocking collectives, shards(): alpha = rr / lax.psum(jnp.sum(d * image), ('gx', 'gy', 'gz'))  583 us
    ppermute x35, starting transfers between devices, extended(): before = lax.ppermute(last, axis, up)  112 us
    ppermute x36, starting transfers between devices, extended(): after = lax.ppermute(first, axis, down)  90.9 us
    ppermute x36, waiting for transfers between devices, extended(): after = lax.ppermute(first, axis, down)  71.4 us
  transfers between devices with their start and end apart: 74, of which 47 were waited for; matrix products, arithmetic and copies ran while one was open for 0% of the time, Pallas kernels for 0%

commit v1 on v0

v1 whole, which is shorter than its diff:
```python
import functools
import itertools

import jax
import jax.numpy as jnp
from jax import lax
from jax.experimental import pallas as pl
from jax.experimental.pallas import tpu as pltpu
from jax.sharding import PartitionSpec as P

CX = 8
CY = 8
CZ = 128
NB = 128
PTS = 128
N = 8
H = 5
EX = CX + 2 * H
LANES = 2 * CZ
AXES = ("gx", "gy", "gz")
MESH = pl.DeviceIdType.MESH
F32 = jnp.float32
BF16 = jnp.bfloat16
C_ALL = 0.25 * (6.0 + 12.0 / 2.0 + 8.0 / 3.0)
SHIFTS = (0.0, 0.85, 0.45, 0.2)
PEERS = (4, 3, 5, 2, 6, 1, 7)
PAIRS = [(i, j) for i in range(4) for j in range(i, 5)]
NEAR = [o for o in itertools.product((-1, 0, 1), repeat=3) if any(o)]


def slot(o):
    return (o[0] + 1) * 9 + (o[1] + 1) * 3 + (o[2] + 1)


def group(dx, dy):
    return (dx + 1) * 3 + (dy + 1)


REACH = {-1: (0, H + 1), 0: (H, CX + 1), 1: (H + CX, H)}
OWNED = {-1: (0, H), 0: (H, CX), 1: (H + CX, H)}
GIVEN = {-1: 0, 0: 0, 1: CX - H}


def two_sum(a, b):
    s = a + b
    t = s - a
    return s, (a - (s - t)) + (b - t)


def quick_sum(a, b):
    s = a + b
    return s, b - (s - a)


def split(a):
    t = a * 4097.0
    high = t - (t - a)
    return high, a - high


def prod_error(p, a, b):
    return ((a[0] * b[0] - p) + a[0] * b[1] + a[1] * b[0]) + a[1] * b[1]


def pair_add(a, b):
    s, e = two_sum(a[0], b[0])
    return quick_sum(s, e + (a[1] + b[1]))


def pair_mul(a, b):
    p = a[0] * b[0]
    e = prod_error(p, split(a[0]), split(b[0]))
    return quick_sum(p, e + (a[0] * b[1] + a[1] * b[0]))


def pair_div(a, b):
    q = a[0] / b[0]
    qb = pair_mul((q, jnp.zeros_like(q)), b)
    r = pair_add(a, (-qb[0], -qb[1]))
    return quick_sum(q, r[0] / b[0])


def coefficients(gram, hi):
    zero = jnp.zeros_like(gram[0][0])
    g = {}
    for e, (i, j) in enumerate(PAIRS):
        g[i, j] = gram[e]
    d, l = [], {}
    for j in range(4):
        piv = g[j, j]
        floor = jnp.maximum(gram[PAIRS.index((j, j))][0] * 1e-13, 1e-36)
        bad = piv[0] < floor
        piv = (jnp.where(bad, floor, piv[0]), jnp.where(bad, zero, piv[1]))
        d.append(piv)
        for k in range(j + 1, 5):
            l[j, k] = pair_div(g[j, k], piv)
        for i in range(j + 1, 4):
            for k in range(i, 5):
                m = pair_mul(l[j, i], g[j, k])
                g[i, k] = pair_add(g[i, k], (-m[0], -m[1]))
    low = {key: val[0] for key, val in l.items()}
    theta = [hi * s for s in SHIFTS]
    tau = [jnp.ones_like(hi)] + [hi * 0.5] * 3
    a = [theta[0] + tau[0] * low[0, 1]]
    for j in (1, 2, 3):
        a.append(theta[j] + (tau[j] * low[j, j + 1] - tau[j - 1] * low[j - 1, j]))
    ratio = [None] + [d[j][0] / d[j - 1][0] for j in (1, 2, 3)]
    c = [jnp.maximum(a[0], 1.0)]
    for j in (1, 2, 3):
        c.append(jnp.maximum(a[j] - tau[j - 1] * tau[j - 1] * ratio[j] / c[j - 1], 1.0))
    f = [jnp.ones_like(hi)]
    for j in (1, 2, 3):
        f.append(-(tau[j - 1] * f[j - 1]) / c[j - 1])
    z = [None] * 4
    z[3] = f[3] / c[3]
    for j in (2, 1, 0):
        z[j] = (f[j] - tau[j] * ratio[j + 1] * z[j + 1]) / c[j]
    y = [None] * 4
    y[3] = z[3]
    y[2] = z[2] - low[2, 3] * y[3]
    y[1] = z[1] - low[1, 2] * y[2] - low[1, 3] * y[3]
    y[0] = z[0] - low[0, 1] * y[1] - low[0, 2] * y[2] - low[0, 3] * y[3]
    return y


def kernel(off, mass, vel, stiff, cell, live, v_out, u_out,
           tr, rx, kt, am, dep, w_s, v0_s, a1_s, a2_s, mb_s, d_s, e_s, f_s, gs, ns, pk, p4,
           v4, zp, rv, rz, ars, arb, ut, vq, qg,
           dep_ss, dep_rs, v_ss, v_rs, ar_ss, ar_rs):
    me = [lax.axis_index(a) for a in AXES]

    def peer(o):
        return tuple(m if q == 0 else lax.rem(m + (q % N), N) for m, q in zip(me, o))

    greeted = set((o[0] % N, o[1] % N, o[2] % N) for o in NEAR)
    for axis in range(3):
        for q in PEERS:
            greeted.add(tuple(q if i == axis else 0 for i in range(3)))
    barrier = pltpu.get_barrier_semaphore()
    for o in sorted(greeted):
        pl.semaphore_signal(barrier, inc=1, device_id=peer(o), device_id_type=MESH)

    row = lax.broadcasted_iota(jnp.int32, (8, LANES), 0)
    low8 = row < 4
    empty = (row & 3) == 3
    low = lax.broadcasted_iota(jnp.int32, (8, 128), 0) < 4
    lane = lax.broadcasted_iota(jnp.int32, (8, 128), 1)
    rows8 = lax.broadcasted_iota(jnp.int32, (8, 128), 0)

    keep = lax.broadcasted_iota(jnp.int32, (PTS, NB), 0) < live[...]
    for i in range(3):
        tr[i] = off[i].T
        tr[3 + i] = vel[i].T
    tr[6] = jnp.where(keep, stiff[...].T, 0.0)
    tr[7] = jnp.where(keep, mass[...].T, 0.0)

    def sums(i, acc):
        at = pl.ds(pl.multiple_of(i * 8, 8), 8)
        fx, fy, fz = tr[0, at], tr[1, at], tr[2, at]
        m = tr[7, at]
        data = [m * tr[3, at], m * tr[4, at], m * tr[5, at], tr[6, at], m]
        new = []
        for wx in (1.0 - fx, fx):
            for wy in (1.0 - fy, fy):
                wxy = wx * wy
                for wz in (1.0 - fz, fz):
                    wt = wxy * wz
                    for value in data:
                        new.append(acc[len(new)] + wt * value)
        return tuple(new)

    acc = lax.fori_loop(0, PTS // 8, sums, tuple(jnp.zeros((8, NB), F32) for _ in range(40)))
    for e in range(40):
        rx[13, e:e + 1, :] = jnp.sum(acc[e], axis=0, keepdims=True)
    rx[13, 40:41, :] = cell[...].astype(F32)
    rx[13, 41:48, :] = jnp.zeros((7, NB), F32)

    pl.semaphore_wait(barrier, len(greeted))

    def neg(o):
        return tuple(-q for q in o)

    def deposit_copy(o):
        return pltpu.make_async_remote_copy(
            src_ref=rx.at[13], dst_ref=rx.at[slot(neg(o))], send_sem=dep_ss.at[slot(o)],
            recv_sem=dep_rs.at[slot(neg(o))], device_id=peer(o), device_id_type=MESH)

    def v_copy(o):
        if o[2] == 0:
            gx0, gy0 = GIVEN[o[0]], GIVEN[o[1]]
            nx, ny = OWNED[-o[0]][1], OWNED[-o[1]][1]
            src = v4.at[pl.ds(gx0, nx), pl.ds(gy0, ny)]
            dst = rv.at[group(-o[0], -o[1]), pl.ds(0, nx), pl.ds(0, ny)]
        else:
            gx0, nx = GIVEN[o[0]], OWNED[-o[0]][1]
            src = zp.at[pl.ds(gx0, nx)]
            dst = rz.at[group(-o[0], -o[1]), (1 - o[2]) // 2, pl.ds(0, nx)]
        return pltpu.make_async_remote_copy(
            src_ref=src, dst_ref=dst, send_sem=v_ss.at[slot(o)], recv_sem=v_rs.at[slot(neg(o))],
            device_id=peer(o), device_id_type=MESH)

    def ar_start(k, p, value):
        ars[k, p] = value
        for j, q in enumerate(PEERS):
            axis = 2 - p
            pltpu.make_async_remote_copy(
                src_ref=ars.at[k, p], dst_ref=arb.at[k, p, j], send_sem=ar_ss.at[k, p],
                recv_sem=ar_rs.at[k, p], device_id=peer(tuple(q if i == axis else 0 for i in range(3))),
                device_id_type=MESH).start()

    def ar_wait(k, p):
        pltpu.make_async_copy(arb.at[k, p], arb.at[k, p], ar_rs.at[k, p]).wait()

    order = sorted(NEAR, key=lambda o: -sum(abs(q) for q in o))
    for o in order:
        deposit_copy(o).start()

    zrow = lax.broadcasted_iota(jnp.int32, (LANES, NB), 0)
    zrow = jnp.where(zrow >= 192, zrow - LANES, zrow)

    def cells(n):
        c = rx[n, 40:41, :].astype(jnp.int32)
        return c >> 10, (c >> 7) & 7, c & 127

    def add_group(dx, dy, zs):
        (x0, nx), (y0, ny) = REACH[dx], REACH[dy]
        width = 256 * len(zs)
        for zi, dz in enumerate(zs):
            n = slot((dx, dy, dz))
            ci, cj, ck = cells(n)
            for c in range(2):
                at = pl.ds((zi * 2 + c) * 128, 128)
                kt[:, at] = jnp.where(zrow == ck + (c + CZ * dz), 1.0, 0.0).astype(BF16)
                u = {}
                ys = {}
                for b in range(2):
                    for yi in range(ny):
                        hit = cj + (b + 8 * dy + H) == y0 + yi
                        ys[b, yi] = jnp.broadcast_to(jnp.where(hit, 1.0, 0.0), (16, NB)).astype(BF16)
                for a in range(2):
                    s16 = []
                    for b in range(2):
                        e = a * 4 + b * 2 + c
                        s = rx[n, 5 * e:5 * e + 8, :]
                        high = s.astype(BF16).astype(F32)
                        s16.append(jnp.concatenate([high, s - high], axis=0).astype(BF16))
                    for yi in range(ny):
                        u[a, yi] = ys[0, yi] * s16[0] + ys[1, yi] * s16[1]

                def plane(xi, _):
                    xs = []
                    for a in range(2):
                        hit = ci + (a + 8 * dx + H) == x0 + xi
                        xs.append(jnp.broadcast_to(jnp.where(hit, 1.0, 0.0), (16, NB)).astype(BF16))
                    for yi in range(ny):
                        am[xi * ny + yi, :, at] = xs[0] * u[0, yi] + xs[1] * u[1, yi]
                    return 0

                lax.fori_loop(0, nx, plane, 0)
        lhs = am[0:nx * ny, :, 0:width].reshape(nx * ny * 16, width)
        out = lax.dot_general(lhs, kt[:, 0:width], (((1,), (1,)), ((), ())), preferred_element_type=F32)
        out = out.reshape(nx, ny, 16, LANES)
        dep[x0:x0 + nx, y0:y0 + ny] += out[:, :, 0:8] + out[:, :, 8:16]

    def clear(x, _):
        dep[x] = jnp.zeros((EX, 8, LANES), F32)
        return 0

    lax.fori_loop(0, EX, clear, 0)
    add_group(0, 0, (0,))

    def node(x, y):
        t = dep[x, y]
        mb = jnp.broadcast_to(dep[x, y, 4:5, :], (8, LANES)) + 1.0
        sb = jnp.broadcast_to(dep[x, y, 3:4, :], (8, LANES)) + 0.1
        dup = jnp.where(low8, t, pltpu.roll(t, 4, 0))
        return jnp.where(empty, 0.0, dup / mb), mb, sb

    def estimate(x, best):
        for y in range(H, H + CY + 1):
            v, mb, sb = node(x, y)
            vv = v * v
            damped = v * (1.0 + 0.6 * vv) / (1.0 + 0.9 * vv)
            vv = jnp.where(low8, vv, damped * damped)
            best = jnp.maximum(best, mb * (1.0 + 0.9 * vv) + 5.0 * sb)
        return best

    best = lax.fori_loop(H, H + CX + 1, estimate, jnp.zeros((8, LANES), F32))
    best = jnp.maximum(best[:, 0:128], best[:, 128:256])
    ar_start(0, 0, best)

    def wait_group(dx, dy):
        for dz in (-1, 0, 1):
            if (dx, dy, dz) != (0, 0, 0):
                deposit_copy((-dx, -dy, -dz)).wait_recv()

    def ar_max(k, p, best):
        ar_wait(k, p)
        for j in range(7):
            best = jnp.maximum(best, arb[k, p, j])
        return best

    wait_group(0, 0)
    add_group(0, 0, (-1, 1))
    best = ar_max(0, 0, best)
    ar_start(0, 1, best)
    groups = [(-1, 0), (1, 0), (0, -1), (0, 1), (-1, -1), (-1, 1), (1, -1), (1, 1)]
    for i, (dx, dy) in enumerate(groups):
        wait_group(dx, dy)
        add_group(dx, dy, (-1, 0, 1))
        if i == 2:
            best = ar_max(0, 1, best)
            ar_start(0, 2, best)

    def coefs(x, _):
        for y in range(EX):
            v, mb, sb = node(x, y)
            a2 = jnp.where(low8, 0.125, 0.125 * sb)
            w_s[x, y] = v
            mb_s[x, y] = mb
            a1_s[x, y] = jnp.where(low8, sb, 1.0)
            a2_s[x, y] = a2
            d_s[x, y] = C_ALL * sb
            f_s[x, y] = jnp.where(row == 3, 0.125 * sb, a2 * v)
        return 0

    lax.fori_loop(0, EX, coefs, 0)

    def level(k, emit):
        first, last = H - k, H + CX + k
        wide = LANES if k else CZ

        def sweep(x, _):
            h = {}
            for y in range(first - 1, last + 1):
                f = f_s[x, y]
                sz = pltpu.roll(f, 1, 1) + pltpu.roll(f, LANES - 1, 1)
                f, sz = f[:, 0:wide], sz[:, 0:wide]
                h[y] = (sz + sz, f + f + sz, f + (2.0 / 3.0) * sz)
                if y - 2 >= first - 1:
                    m = y - 1
                    gs[x, m, :, 0:wide] = h[m][1] + (h[m - 1][2] + h[m + 1][2])
                    ns[x, m, :, 0:wide] = h[m][0] + (h[m - 1][1] + h[m + 1][1])
            return 0

        lax.fori_loop(first - 1, last + 1, sweep, 0)

        def combine(x, _):
            for y in range(first, last):
                emit(x, y, ns[x, y, :, 0:wide] + (gs[x - 1, y, :, 0:wide] + gs[x + 1, y, :, 0:wide]))
            return 0

        lax.fori_loop(first, last, combine, 0)

    def folded(x, y, sums, wide):
        q = a1_s[x, y, :, 0:wide] * sums
        return q + pltpu.roll(q, 4, 0)

    def first_residual(x, y, sums):
        d = d_s[x, y] + jnp.broadcast_to(sums[3:4, :], (8, LANES))
        d_s[x, y] = d
        lq = folded(x, y, sums, LANES)
        v = w_s[x, y]
        mb = mb_s[x, y]
        mvv = mb * v * v
        e_s[x, y] = mb + 0.9 * mvv + d
        p = jnp.where(empty, 0.0, lq - (d + 0.3 * mvv) * v)
        pk[0, x, y] = p
        f_s[x, y] = a2_s[x, y] * p

    def second_residual(x, y, sums):
        d = d_s[x, y]
        lq = folded(x, y, sums, LANES)
        v = w_s[x, y]
        mb = mb_s[x, y]
        mvv = mb * v * v
        e_s[x, y] = mb + 0.9 * mvv + d
        p = lq - (d + 0.3 * mvv) * v - mb * (v - v0_s[x, y])
        pk[0, x, y] = p
        f_s[x, y] = a2_s[x, y] * p

    def basis(k, hi):
        theta = hi * SHIFTS[k]
        inv = 2.0 / hi
        wide = CZ if k == 3 else LANES
        theta = jnp.broadcast_to(theta, (8, wide))
        inv = jnp.broadcast_to(inv, (8, wide))

        def emit(x, y, sums):
            lq = folded(x, y, sums, wide)
            e = e_s[x, y, :, 0:wide]
            if k:
                e = e - theta
            p = e * pk[k, x, y, :, 0:wide] - lq
            if k:
                p = p * inv
            if k == 3:
                p4[x - H, y - H] = p
            else:
                pk[k + 1, x, y] = p
                f_s[x, y] = a2_s[x, y] * p

        level(3 - k, emit)

    def gram():
        def plane(x, carry):
            acc = list(carry)
            for y in range(4):
                p = [jnp.where(low, pk[i, H + x, H + y, :, 0:128], pk[i, H + x, H + 4 + y, :, 0:128]) for i in range(4)]
                p.append(jnp.where(low, p4[x, y], p4[x, y + 4]))
                parts = [split(q) for q in p]
                for e, (i, j) in enumerate(PAIRS):
                    m = p[i] * p[j]
                    err = prod_error(m, parts[i], parts[j])
                    s, t = two_sum(acc[2 * e], m)
                    acc[2 * e] = s
                    acc[2 * e + 1] = acc[2 * e + 1] + (t + err)
            return tuple(acc)

        acc = lax.fori_loop(0, CX, plane, tuple(jnp.zeros((8, 128), F32) for _ in range(28)))
        packed = []
        for part in range(2):
            high = jnp.zeros((8, 128), F32)
            rest = jnp.zeros((8, 128), F32)
            for r in range(8):
                e = part * 8 + r
                if e >= 14:
                    continue
                a = (acc[2 * e], acc[2 * e + 1])
                for s in (4, 2, 1):
                    a = pair_add(a, (pltpu.roll(a[0], s, 0), pltpu.roll(a[1], s, 0)))
                high = jnp.where(rows8 == r, a[0], high)
                rest = jnp.where(rows8 == r, a[1], rest)
            a = (high, rest)
            for s in (64, 32, 16, 8, 4, 2, 1):
                a = pair_add(a, (pltpu.roll(a[0], s, 1), pltpu.roll(a[1], s, 1)))
            packed.append(a)
        return jnp.where(lane < 32, packed[0][0], jnp.where(lane < 64, packed[0][1], jnp.where(lane < 96, packed[1][0], packed[1][1])))

    even = (lane & 32) == 0

    def ar_sum(k, p, own):
        ar_wait(k, p)
        total = (own, pltpu.roll(own, 96, 1))
        for j in range(7):
            other = arb[k, p, j]
            total = pair_add(total, (other, pltpu.roll(other, 96, 1)))
        return jnp.where(even, total[0], pltpu.roll(total[1], 32, 1))

    def solve(k, hi):
        g = gram()
        for p in range(3):
            ar_start(k, p, g)
            g = ar_sum(k, p, g)
        entries = []
        for e in range(14):
            r, base = e % 8, 64 * (e // 8)
            entries.append(tuple(jnp.broadcast_to(g[r:r + 1, base + s:base + s + 1], (8, 128)) for s in (0, 32)))
        return coefficients(entries, hi)

    first_hi = None
    level(4, first_residual)
    basis(0, jnp.ones((1, 1), F32))
    best = ar_max(0, 2, best)
    hi1 = jnp.max(jnp.max(jnp.where(low, best, 0.0), axis=0, keepdims=True), axis=1, keepdims=True)
    hi2 = jnp.max(jnp.max(jnp.where(low, 0.0, best), axis=0, keepdims=True), axis=1, keepdims=True)
    for k in (1, 2, 3):
        basis(k, hi1)
    y1 = solve(1, jnp.broadcast_to(hi1, (8, 128)))

    slots = [(lane >= 16 * y - 5) & (lane < 16 * y + 5) for y in range(8)]
    slots[0] = (lane < 5) | (lane >= 123)

    def update(x, _):
        packed = jnp.zeros((8, 128), F32)
        for y in range(CY):
            v = w_s[H + x, H + y, :, 0:128]
            for i in range(4):
                v = v + y1[i] * pk[i, H + x, H + y, :, 0:128]
            v4[x, y] = v[0:4, :]
            w_s[H + x, H + y, :, 0:128] = v
            packed = jnp.where(slots[y], pltpu.roll(v, (16 * y) % 128, 1) if y else v, packed)
        zp[x] = packed[0:4, :]
        return 0

    def keep_target(x, _):
        for y in range(1, EX - 1):
            v0_s[x, y] = w_s[x, y]
        return 0

    lax.fori_loop(1, EX - 1, keep_target, 0)
    lax.fori_loop(0, CX, update, 0)
    for o in order:
        v_copy(o).start()

    near_low = (lane & 15) < 8

    def take(dx, dy):
        (x0, nx), (y0, ny) = OWNED[dx], OWNED[dy]
        gy0 = GIVEN[-dy]
        g = group(dx, dy)
        for dz in (-1, 0, 1):
            if (dx, dy, dz) != (0, 0, 0):
                v_copy((-dx, -dy, -dz)).wait_recv()

        def plane(x, _):
            after = rz[g, 1, x]
            before = rz[g, 0, x]
            after = jnp.concatenate([after, after], axis=0)
            before = jnp.concatenate([before, before], axis=0)
            ends = jnp.where(near_low, after, before)
            for y in range(ny):
                sy = (128 - 16 * (gy0 + y)) % 128
                tail = pltpu.roll(ends, sy, 1) if sy else ends
                w_s[x0 + x, y0 + y, :, 128:256] = tail
                f_s[x0 + x, y0 + y, :, 128:256] = a2_s[x0 + x, y0 + y, :, 128:256] * tail
                if (dx, dy) == (0, 0):
                    head = w_s[x0 + x, y0 + y, :, 0:128]
                else:
                    head = rv[g, x, y]
                    head = jnp.concatenate([head, head], axis=0)
                    w_s[x0 + x, y0 + y, :, 0:128] = head
                f_s[x0 + x, y0 + y, :, 0:128] = a2_s[x0 + x, y0 + y, :, 0:128] * head
            return 0

        lax.fori_loop(0, nx, plane, 0)

    take(0, 0)
    for dx, dy in groups:
        take(dx, dy)

    level(4, second_residual)
    for k in range(4):
        basis(k, hi2)
    y2 = solve(2, jnp.broadcast_to(hi2, (8, 128)))
    y2 = [jnp.concatenate([q, q], axis=1) for q in y2]

    def finish(x, _):
        for y in range(CY + 1):
            v = w_s[H + x, H + y]
            for i in range(4):
                v = v + y2[i] * pk[i, H + x, H + y]
            w_s[H + x, H + y] = v
            high = v.astype(BF16).astype(F32)
            vq[x * 9 + y] = jnp.where(low8, high, v - high)
        return 0

    lax.fori_loop(0, CX + 1, finish, 0)
    for f in range(3):
        for x in range(CX):
            for y in range(CY):
                v_out[f, x, y:y + 1, :] = w_s[H + x, H + y, f:f + 1, 0:128]

    ci, cj, ck = cells(13)
    for c in range(2):
        kt[:, c * 128:(c + 1) * 128] = jnp.where(zrow == ck + c, 1.0, 0.0).astype(BF16)
    qg[...] = jnp.dot(vq[...].reshape(81 * 8, LANES).astype(BF16), kt[:, 0:256],
                      preferred_element_type=F32).reshape(81, 8, LANES)
    ci = jnp.broadcast_to(jnp.concatenate([ci, ci], axis=1), (8, LANES))
    cj = jnp.broadcast_to(jnp.concatenate([cj, cj], axis=1), (8, LANES))
    corner = {}
    for a in range(2):
        at_x = []
        for y in range(9):
            z = qg[a * 9 + y]
            for x in range(1, 8):
                z = jnp.where(ci == x, qg[(x + a) * 9 + y], z)
            at_x.append(z)
        for b in range(2):
            z = at_x[b]
            for y in range(1, 8):
                z = jnp.where(cj == y, at_x[y + b], z)
            corner[a, b] = z + pltpu.roll(z, 4, 0)

    def points(i, _):
        at = pl.ds(pl.multiple_of(i * 8, 8), 8)
        fx, fy, fz = tr[0, at], tr[1, at], tr[2, at]
        gx, gy, gz = 1.0 - fx, 1.0 - fy, 1.0 - fz
        w = {(0, 0): gx * gy, (0, 1): gx * fy, (1, 0): fx * gy, (1, 1): fx * fy}
        for f in range(3):
            total = None
            for key, wt in w.items():
                r = corner[key]
                term = wt * (gz * r[f:f + 1, 0:128] + fz * r[f:f + 1, 128:256])
                total = term if total is None else total + term
            ut[f, at] = total
        return 0

    lax.fori_loop(0, PTS // 8, points, 0)
    for f in range(3):
        u_out[f] = ut[f].T

    for o in order:
        deposit_copy(o).wait_send()
        v_copy(o).wait_send()
    for k in range(3):
        for p in range(3):
            pltpu.make_async_copy(arb.at[k, p], arb.at[k, p], ar_ss.at[k, p]).wait()


def shards(point_offset, point_mass, point_velocity, point_stiffness, cell_index, live_count):
    vm = pl.BlockSpec(memory_space=pltpu.VMEM)
    ext = pltpu.VMEM((EX, EX, 8, LANES), F32)
    v, u = pl.pallas_call(
        kernel,
        out_shape=(jax.ShapeDtypeStruct((3, CX, CY, CZ), F32), jax.ShapeDtypeStruct((3, NB, PTS), F32)),
        in_specs=[vm] * 6,
        out_specs=(vm, vm),
        scratch_shapes=[
            pltpu.VMEM((8, PTS, NB), F32),
            pltpu.VMEM((27, 48, NB), F32),
            pltpu.VMEM((LANES, 768), BF16),
            pltpu.VMEM((81, 16, 768), BF16),
            ext, ext, ext, ext, ext, ext, ext, ext, ext, ext, ext,
            pltpu.VMEM((4, EX, EX, 8, LANES), F32),
            pltpu.VMEM((CX, CY, 8, CZ), F32),
            pltpu.VMEM((CX, CY, 4, CZ), F32),
            pltpu.VMEM((CX, 4, CZ), F32),
            pltpu.VMEM((9, CX, CY, 4, CZ), F32),
            pltpu.VMEM((9, 2, CX, 4, CZ), F32),
            pltpu.VMEM((3, 3, 8, 128), F32),
            pltpu.VMEM((3, 3, 7, 8, 128), F32),
            pltpu.VMEM((3, PTS, NB), F32),
            pltpu.VMEM((81, 8, LANES), F32),
            pltpu.VMEM((81, 8, LANES), F32),
            pltpu.SemaphoreType.DMA((27,)),
            pltpu.SemaphoreType.DMA((27,)),
            pltpu.SemaphoreType.DMA((27,)),
            pltpu.SemaphoreType.DMA((27,)),
            pltpu.SemaphoreType.DMA((3, 3)),
            pltpu.SemaphoreType.DMA((3, 3)),
        ],
        compiler_params=pltpu.CompilerParams(
            collective_id=0, has_side_effects=True, vmem_limit_bytes=60 << 20),
        name="granular_step",
    )(
        point_offset.reshape(3, NB, PTS),
        point_mass.reshape(NB, PTS),
        point_velocity.reshape(3, NB, PTS),
        point_stiffness.reshape(NB, PTS),
        cell_index.reshape(1, NB),
        live_count.reshape(1, NB),
    )
    return v, u.reshape(3, 1, 1, 1, NB, PTS)


def solution(mesh):
    return jax.shard_map(
        shards,
        mesh=mesh,
        in_specs=(
            P(None, "gx", "gy", "gz", None, None),
            P("gx", "gy", "gz", None, None),
            P(None, "gx", "gy", "gz", None, None),
            P("gx", "gy", "gz", None, None),
            P("gx", "gy", "gz", None),
            P("gx", "gy", "gz", None),
        ),
        out_specs=(P(None, "gx", "gy", "gz"), P(None, "gx", "gy", "gz", None, None)),
        check_vma=False,
    )
```

time: 1810 us -> 105 us (0.06)
  the two profiles are of different devices: /device:TPU:25 before, /device:TPU:2 now
where the time goes in v1:
time: 105 us
  Pallas kernels  102 us (97%)
  local copies, waits for them, and re-layouts  2.26 us (2%)
    pallas_call x1, Pallas kernels, shards(): pl.pallas_call(kernel, out_shape=(jax.ShapeDtypeStruct((3, CX, CY, CZ), F...  102 us
    unnamed x4, local copies, waits for them, and re-layouts  2.26 us

profile of v1, /device:TPU:2, one launch (start us, length us, event | category | flops | bytes accessed | tf_op | source)
XLA Modules:
  0.0 105.2 jit_solution(3685707828789853896)
XLA Ops:
  0.6 102.3 %granular_step.1 = (f32[3,8,8,128]{3,2,1,0:T(8,128)}, f32[3,128,128]{2,1,0:T(8,128)}) custom-call(f32[3,128,128]{2,1,0:T(8,128)} %bitcast.10, f32[128,128]{1,0:T(8,128)} %bitcast.12, f32[3,128,128]{2,1,0:T(8,128)} %bitcast.11, f32[128,128]{1,0:T(8,128)} %bitcast.13, s32[1,128]{1,0:T(1,128)} %bitcast.14, s32[1,128]{1,0:T(1,128)} %bitcast.15), custom_call_target="tpu_custom_call" | custom-call | tf_op jit(solution)/shard_map/granular_step/pallas_call | solution.py:604
  102.9 0.0 copy-start
  102.9 1.6 %copy.11 = f32[3,8,8,128]{3,2,1,0:T(8,128)} copy(f32[3,8,8,128]{3,2,1,0:T(8,128)} %get-tuple-element.10) | data formatting | bytes 196608
  104.5 0.0 copy-done
  104.5 0.7 copy.12
Async XLA Ops:
  102.9 1.6 %copy-start = (f32[3,128,128]{2,1,0:T(8,128)S(1)}, f32[3,128,128]{2,1,0:T(8,128)}, u32[]{:S(2)}) copy-start(f32[3,128,128]{2,1,0:T(8,128)} %get-tuple-element.5) | copy-start | bytes 589828

commit v2 on v1

--- a/solution.py
+++ b/solution.py
@@ -124,10 +124,11 @@
 
 
 def kernel(off, mass, vel, stiff, cell, live, v_out, u_out,
-           tr, rx, kt, am, dep, w_s, v0_s, a1_s, a2_s, mb_s, d_s, e_s, f_s, gs, ns, pk, p4,
+           tr, rx, kt0, kt1, am0, am1, dep, w_s, v0_s, a1_s, a2_s, mb_s, d_s, e_s, f_s, gs, ns, pk, p4,
            v4, zp, rv, rz, ars, arb, ut, vq, qg,
            dep_ss, dep_rs, v_ss, v_rs, ar_ss, ar_rs):
     me = [lax.axis_index(a) for a in AXES]
+    kts, ams = (kt0, kt1), (am0, am1)
 
     def peer(o):
         return tuple(m if q == 0 else lax.rem(m + (q % N), N) for m, q in zip(me, o))
@@ -200,7 +201,8 @@
             device_id=peer(o), device_id_type=MESH)
 
     def ar_start(k, p, value):
-        ars[k, p] = value
+        ars[k, p, 0:8] = value[0]
+        ars[k, p, 8:16] = value[1]
         for j, q in enumerate(PEERS):
             axis = 2 - p
             pltpu.make_async_remote_copy(
@@ -222,7 +224,8 @@
         c = rx[n, 40:41, :].astype(jnp.int32)
         return c >> 10, (c >> 7) & 7, c & 127
 
-    def add_group(dx, dy, zs):
+    def add_group(dx, dy, zs, which):
+        kt, am = kts[which], ams[which]
         (x0, nx), (y0, ny) = REACH[dx], REACH[dy]
         width = 256 * len(zs)
         for zi, dz in enumerate(zs):
@@ -231,63 +234,50 @@
             for c in range(2):
                 at = pl.ds((zi * 2 + c) * 128, 128)
                 kt[:, at] = jnp.where(zrow == ck + (c + CZ * dz), 1.0, 0.0).astype(BF16)
-                u = {}
-                ys = {}
+                ys, xs = [], []
                 for b in range(2):
-                    for yi in range(ny):
-                        hit = cj + (b + 8 * dy + H) == y0 + yi
-                        ys[b, yi] = jnp.broadcast_to(jnp.where(hit, 1.0, 0.0), (16, NB)).astype(BF16)
+                    plane = lax.broadcasted_iota(jnp.int32, (ny, 16, NB), 0)
+                    ys.append(jnp.where(plane == cj + (b + 8 * dy + H - y0), 1.0, 0.0).astype(BF16))
+                    plane = lax.broadcasted_iota(jnp.int32, (nx, 16, NB), 0)
+                    xs.append(jnp.where(plane == ci + (b + 8 * dx + H - x0), 1.0, 0.0).astype(BF16))
+                total = None
                 for a in range(2):
-                    s16 = []
+                    u = None
                     for b in range(2):
                         e = a * 4 + b * 2 + c
                         s = rx[n, 5 * e:5 * e + 8, :]
                         high = s.astype(BF16).astype(F32)
-                        s16.append(jnp.concatenate([high, s - high], axis=0).astype(BF16))
-                    for yi in range(ny):
-                        u[a, yi] = ys[0, yi] * s16[0] + ys[1, yi] * s16[1]
-
-                def plane(xi, _):
-                    xs = []
-                    for a in range(2):
-                        hit = ci + (a + 8 * dx + H) == x0 + xi
-                        xs.append(jnp.broadcast_to(jnp.where(hit, 1.0, 0.0), (16, NB)).astype(BF16))
-                    for yi in range(ny):
-                        am[xi * ny + yi, :, at] = xs[0] * u[0, yi] + xs[1] * u[1, yi]
-                    return 0
-
-                lax.fori_loop(0, nx, plane, 0)
+                        s16 = jnp.concatenate([high, s - high], axis=0).astype(BF16)
+                        term = ys[b] * s16
+                        u = term if u is None else u + term
+                    term = xs[a].reshape(nx, 1, 16, NB) * u.reshape(1, ny, 16, NB)
+                    total = term if total is None else total + term
+                am[0:nx * ny, :, at] = total.reshape(nx * ny, 16, NB)
         lhs = am[0:nx * ny, :, 0:width].reshape(nx * ny * 16, width)
         out = lax.dot_general(lhs, kt[:, 0:width], (((1,), (1,)), ((), ())), preferred_element_type=F32)
         out = out.reshape(nx, ny, 16, LANES)
         dep[x0:x0 + nx, y0:y0 + ny] += out[:, :, 0:8] + out[:, :, 8:16]
 
-    def clear(x, _):
-        dep[x] = jnp.zeros((EX, 8, LANES), F32)
-        return 0
-
-    lax.fori_loop(0, EX, clear, 0)
-    add_group(0, 0, (0,))
-
-    def node(x, y):
-        t = dep[x, y]
-        mb = jnp.broadcast_to(dep[x, y, 4:5, :], (8, LANES)) + 1.0
-        sb = jnp.broadcast_to(dep[x, y, 3:4, :], (8, LANES)) + 0.1
-        dup = jnp.where(low8, t, pltpu.roll(t, 4, 0))
+    dep[...] = jnp.zeros((EX, EX, 8, LANES), F32)
+    add_group(0, 0, (0,), 1)
+
+    def node(x, ys):
+        t = dep[x, ys]
+        mb = jnp.broadcast_to(dep[x, ys, 4:5, :], t.shape) + 1.0
+        sb = jnp.broadcast_to(dep[x, ys, 3:4, :], t.shape) + 0.1
+        dup = jnp.where(low8, t, pltpu.roll(t, 4, 1))
         return jnp.where(empty, 0.0, dup / mb), mb, sb
 
     def estimate(x, best):
-        for y in range(H, H + CY + 1):
-            v, mb, sb = node(x, y)
-            vv = v * v
-            damped = v * (1.0 + 0.6 * vv) / (1.0 + 0.9 * vv)
-            vv = jnp.where(low8, vv, damped * damped)
-            best = jnp.maximum(best, mb * (1.0 + 0.9 * vv) + 5.0 * sb)
-        return best
+        v, mb, sb = node(x, pl.ds(H, CY + 1))
+        vv = v * v
+        damped = v * (1.0 + 0.6 * vv) / (1.0 + 0.9 * vv)
+        vv = jnp.where(low8, vv, damped * damped)
+        return jnp.maximum(best, jnp.max(mb * (1.0 + 0.9 * vv) + 5.0 * sb, axis=0))
 
     best = lax.fori_loop(H, H + CX + 1, estimate, jnp.zeros((8, LANES), F32))
     best = jnp.maximum(best[:, 0:128], best[:, 128:256])
-    ar_start(0, 0, best)
+    ar_start(0, 0, (best, best))
 
     def wait_group(dx, dy):
         for dz in (-1, 0, 1):
@@ -297,108 +287,97 @@
     def ar_max(k, p, best):
         ar_wait(k, p)
         for j in range(7):
-            best = jnp.maximum(best, arb[k, p, j])
+            best = jnp.maximum(best, arb[k, p, j, 0:8])
         return best
 
+    best = ar_max(0, 0, best)
+    ar_start(0, 1, (best, best))
     wait_group(0, 0)
-    add_group(0, 0, (-1, 1))
-    best = ar_max(0, 0, best)
-    ar_start(0, 1, best)
+    add_group(0, 0, (-1, 1), 0)
     groups = [(-1, 0), (1, 0), (0, -1), (0, 1), (-1, -1), (-1, 1), (1, -1), (1, 1)]
     for i, (dx, dy) in enumerate(groups):
         wait_group(dx, dy)
-        add_group(dx, dy, (-1, 0, 1))
-        if i == 2:
+        add_group(dx, dy, (-1, 0, 1), (i + 1) % 2)
+        if i == 4:
             best = ar_max(0, 1, best)
-            ar_start(0, 2, best)
+            ar_start(0, 2, (best, best))
 
     def coefs(x, _):
-        for y in range(EX):
-            v, mb, sb = node(x, y)
-            a2 = jnp.where(low8, 0.125, 0.125 * sb)
-            w_s[x, y] = v
-            mb_s[x, y] = mb
-            a1_s[x, y] = jnp.where(low8, sb, 1.0)
-            a2_s[x, y] = a2
-            d_s[x, y] = C_ALL * sb
-            f_s[x, y] = jnp.where(row == 3, 0.125 * sb, a2 * v)
+        v, mb, sb = node(x, pl.ds(0, EX))
+        a2 = jnp.where(low8, 0.125, 0.125 * sb)
+        w_s[x] = v
+        mb_s[x] = mb
+        a1_s[x] = jnp.where(low8, sb, 1.0)
+        a2_s[x] = a2
+        d_s[x] = C_ALL * sb
+        f_s[x] = jnp.where(row == 3, 0.125 * sb, a2 * v)
         return 0
 
     lax.fori_loop(0, EX, coefs, 0)
 
     def level(k, emit):
         first, last = H - k, H + CX + k
-        wide = LANES if k else CZ
-
-        def sweep(x, _):
-            h = {}
-            for y in range(first - 1, last + 1):
-                f = f_s[x, y]
-                sz = pltpu.roll(f, 1, 1) + pltpu.roll(f, LANES - 1, 1)
-                f, sz = f[:, 0:wide], sz[:, 0:wide]
-                h[y] = (sz + sz, f + f + sz, f + (2.0 / 3.0) * sz)
-                if y - 2 >= first - 1:
-                    m = y - 1
-                    gs[x, m, :, 0:wide] = h[m][1] + (h[m - 1][2] + h[m + 1][2])
-                    ns[x, m, :, 0:wide] = h[m][0] + (h[m - 1][1] + h[m + 1][1])
-            return 0
-
-        lax.fori_loop(first - 1, last + 1, sweep, 0)
-
-        def combine(x, _):
-            for y in range(first, last):
-                emit(x, y, ns[x, y, :, 0:wide] + (gs[x - 1, y, :, 0:wide] + gs[x + 1, y, :, 0:wide]))
-            return 0
-
-        lax.fori_loop(first, last, combine, 0)
-
-    def folded(x, y, sums, wide):
-        q = a1_s[x, y, :, 0:wide] * sums
-        return q + pltpu.roll(q, 4, 0)
-
-    def first_residual(x, y, sums):
-        d = d_s[x, y] + jnp.broadcast_to(sums[3:4, :], (8, LANES))
-        d_s[x, y] = d
-        lq = folded(x, y, sums, LANES)
-        v = w_s[x, y]
-        mb = mb_s[x, y]
+        ys = pl.ds(first, last - first)
+        wide = pl.ds(0, LANES if k else CZ)
+        for x in range(first - 1, last + 1):
+            f = f_s[x, first - 1:last + 1]
+            sz = pltpu.roll(f, 1, 2) + pltpu.roll(f, LANES - 1, 2)
+            if not k:
+                f, sz = f[:, :, 0:CZ], sz[:, :, 0:CZ]
+            h0, h1, h2 = sz + sz, f + f + sz, f + (2.0 / 3.0) * sz
+            gs[x, ys, :, wide] = h1[1:-1] + (h2[:-2] + h2[2:])
+            ns[x, ys, :, wide] = h0[1:-1] + (h1[:-2] + h1[2:])
+        for x in range(first, last):
+            emit(x, ys, ns[x, ys, :, wide] + (gs[x - 1, ys, :, wide] + gs[x + 1, ys, :, wide]))
+
+    def folded(x, ys, sums, wide):
+        q = a1_s[x, ys, :, wide] * sums
+        return q + pltpu.roll(q, 4, 1)
+
+    full = pl.ds(0, LANES)
+
+    def first_residual(x, ys, sums):
+        d = d_s[x, ys] + jnp.broadcast_to(sums[:, 3:4, :], sums.shape)
+        d_s[x, ys] = d
+        lq = folded(x, ys, sums, full)
+        v = w_s[x, ys]
+        mb = mb_s[x, ys]
         mvv = mb * v * v
-        e_s[x, y] = mb + 0.9 * mvv + d
+        e_s[x, ys] = mb + 0.9 * mvv + d
         p = jnp.where(empty, 0.0, lq - (d + 0.3 * mvv) * v)
-        pk[0, x, y] = p
-        f_s[x, y] = a2_s[x, y] * p
-
-    def second_residual(x, y, sums):
-        d = d_s[x, y]
-        lq = folded(x, y, sums, LANES)
-        v = w_s[x, y]
-        mb = mb_s[x, y]
+        pk[0, x, ys] = p
+        f_s[x, ys] = a2_s[x, ys] * p
+
+    def second_residual(x, ys, sums):
+        d = d_s[x, ys]
+        lq = folded(x, ys, sums, full)
+        v = w_s[x, ys]
+        mb = mb_s[x, ys]
         mvv = mb * v * v
-        e_s[x, y] = mb + 0.9 * mvv + d
-        p = lq - (d + 0.3 * mvv) * v - mb * (v - v0_s[x, y])
-        pk[0, x, y] = p
-        f_s[x, y] = a2_s[x, y] * p
+        e_s[x, ys] = mb + 0.9 * mvv + d
+        p = lq - (d + 0.3 * mvv) * v - mb * (v - v0_s[x, ys])
+        pk[0, x, ys] = p
+        f_s[x, ys] = a2_s[x, ys] * p
 
     def basis(k, hi):
-        theta = hi * SHIFTS[k]
-        inv = 2.0 / hi
-        wide = CZ if k == 3 else LANES
-        theta = jnp.broadcast_to(theta, (8, wide))
-        inv = jnp.broadcast_to(inv, (8, wide))
-
-        def emit(x, y, sums):
-            lq = folded(x, y, sums, wide)
-            e = e_s[x, y, :, 0:wide]
+        lanes = CZ if k == 3 else LANES
+        wide = pl.ds(0, lanes)
+        theta = jnp.broadcast_to(hi * SHIFTS[k], (8, lanes))
+        inv = jnp.broadcast_to(2.0 / hi, (8, lanes))
+
+        def emit(x, ys, sums):
+            lq = folded(x, ys, sums, wide)
+            e = e_s[x, ys, :, wide]
             if k:
                 e = e - theta
-            p = e * pk[k, x, y, :, 0:wide] - lq
+            p = e * pk[k, x, ys, :, wide] - lq
             if k:
                 p = p * inv
             if k == 3:
-                p4[x - H, y - H] = p
+                p4[x - H] = p
             else:
-                pk[k + 1, x, y] = p
-                f_s[x, y] = a2_s[x, y] * p
+                pk[k + 1, x, ys] = p
+                f_s[x, ys] = a2_s[x, ys] * p
 
         level(3 - k, emit)
 
@@ -417,7 +396,7 @@
                     acc[2 * e + 1] = acc[2 * e + 1] + (t + err)
             return tuple(acc)
 
-        acc = lax.fori_loop(0, CX, plane, tuple(jnp.zeros((8, 128), F32) for _ in range(28)))
+        acc = lax.fori_loop(0, CX, plane, tuple(jnp.zeros((8, 128), F32) for _ in range(28)), unroll=2)
         packed = []
         for part in range(2):
             high = jnp.zeros((8, 128), F32)
@@ -435,30 +414,28 @@
             for s in (64, 32, 16, 8, 4, 2, 1):
                 a = pair_add(a, (pltpu.roll(a[0], s, 1), pltpu.roll(a[1], s, 1)))
             packed.append(a)
-        return jnp.where(lane < 32, packed[0][0], jnp.where(lane < 64, packed[0][1], jnp.where(lane < 96, packed[1][0], packed[1][1])))
-
-    even = (lane & 32) == 0
+        return tuple(jnp.where(lane < 64, packed[0][i], packed[1][i]) for i in range(2))
 
     def ar_sum(k, p, own):
         ar_wait(k, p)
-        total = (own, pltpu.roll(own, 96, 1))
-        for j in range(7):
-            other = arb[k, p, j]
-            total = pair_add(total, (other, pltpu.roll(other, 96, 1)))
-        return jnp.where(even, total[0], pltpu.roll(total[1], 32, 1))
-
-    def solve(k, hi):
+        terms = [own] + [(arb[k, p, j, 0:8], arb[k, p, j, 8:16]) for j in range(7)]
+        while len(terms) > 1:
+            terms = [pair_add(terms[i], terms[i + 1]) for i in range(0, len(terms), 2)]
+        return terms[0]
+
+    def solve(k, hi, idle):
         g = gram()
         for p in range(3):
             ar_start(k, p, g)
+            if p == 0:
+                idle()
             g = ar_sum(k, p, g)
         entries = []
         for e in range(14):
             r, base = e % 8, 64 * (e // 8)
-            entries.append(tuple(jnp.broadcast_to(g[r:r + 1, base + s:base + s + 1], (8, 128)) for s in (0, 32)))
+            entries.append(tuple(jnp.broadcast_to(q[r:r + 1, base:base + 1], (8, 128)) for q in g))
         return coefficients(entries, hi)
 
-    first_hi = None
     level(4, first_residual)
     basis(0, jnp.ones((1, 1), F32))
     best = ar_max(0, 2, best)
@@ -466,30 +443,33 @@
     hi2 = jnp.max(jnp.max(jnp.where(low, 0.0, best), axis=0, keepdims=True), axis=1, keepdims=True)
     for k in (1, 2, 3):
         basis(k, hi1)
-    y1 = solve(1, jnp.broadcast_to(hi1, (8, 128)))
+    def keep_target():
+        def plane(x, _):
+            v0_s[x] = w_s[x]
+            return 0
+
+        lax.fori_loop(1, EX - 1, plane, 0)
+
+    y1 = solve(1, jnp.broadcast_to(hi1, (8, 128)), keep_target)
 
     slots = [(lane >= 16 * y - 5) & (lane < 16 * y + 5) for y in range(8)]
     slots[0] = (lane < 5) | (lane >= 123)
 
     def update(x, _):
-        packed = jnp.zeros((8, 128), F32)
-        for y in range(CY):
-            v = w_s[H + x, H + y, :, 0:128]
-            for i in range(4):
-                v = v + y1[i] * pk[i, H + x, H + y, :, 0:128]
-            v4[x, y] = v[0:4, :]
-            w_s[H + x, H + y, :, 0:128] = v
-            packed = jnp.where(slots[y], pltpu.roll(v, (16 * y) % 128, 1) if y else v, packed)
+        ys = pl.ds(H, CY)
+        v = w_s[H + x, ys, :, 0:128]
+        for i in range(4):
+            v = v + y1[i] * pk[i, H + x, ys, :, 0:128]
+        w_s[H + x, ys, :, 0:128] = v
+        v4[x] = v[:, 0:4, :]
+        packed = v[0]
+        for y in range(1, CY):
+            packed = jnp.where(slots[y], pltpu.roll(v[y], 16 * y, 1), packed)
         zp[x] = packed[0:4, :]
         return 0
 
-    def keep_target(x, _):
-        for y in range(1, EX - 1):
-            v0_s[x, y] = w_s[x, y]
-        return 0
-
-    lax.fori_loop(1, EX - 1, keep_target, 0)
-    lax.fori_loop(0, CX, update, 0)
+    for x in range(CX):
+        update(x, 0)
     for o in order:
         v_copy(o).start()
 
@@ -511,19 +491,16 @@
             ends = jnp.where(near_low, after, before)
             for y in range(ny):
                 sy = (128 - 16 * (gy0 + y)) % 128
-                tail = pltpu.roll(ends, sy, 1) if sy else ends
-                w_s[x0 + x, y0 + y, :, 128:256] = tail
-                f_s[x0 + x, y0 + y, :, 128:256] = a2_s[x0 + x, y0 + y, :, 128:256] * tail
-                if (dx, dy) == (0, 0):
-                    head = w_s[x0 + x, y0 + y, :, 0:128]
-                else:
-                    head = rv[g, x, y]
-                    head = jnp.concatenate([head, head], axis=0)
-                    w_s[x0 + x, y0 + y, :, 0:128] = head
-                f_s[x0 + x, y0 + y, :, 0:128] = a2_s[x0 + x, y0 + y, :, 0:128] * head
+                w_s[x0 + x, y0 + y, :, 128:256] = pltpu.roll(ends, sy, 1) if sy else ends
+            ys = pl.ds(y0, ny)
+            if (dx, dy) != (0, 0):
+                head = rv[g, x, 0:ny]
+                w_s[x0 + x, ys, :, 0:128] = jnp.concatenate([head, head], axis=1)
+            f_s[x0 + x, ys] = a2_s[x0 + x, ys] * w_s[x0 + x, ys]
             return 0
 
-        lax.fori_loop(0, nx, plane, 0)
+        for x in range(nx):
+            plane(x, 0)
 
     take(0, 0)
     for dx, dy in groups:
@@ -532,20 +509,21 @@
     level(4, second_residual)
     for k in range(4):
         basis(k, hi2)
-    y2 = solve(2, jnp.broadcast_to(hi2, (8, 128)))
+    y2 = solve(2, jnp.broadcast_to(hi2, (8, 128)), lambda: None)
     y2 = [jnp.concatenate([q, q], axis=1) for q in y2]
 
     def finish(x, _):
-        for y in range(CY + 1):
-            v = w_s[H + x, H + y]
-            for i in range(4):
-                v = v + y2[i] * pk[i, H + x, H + y]
-            w_s[H + x, H + y] = v
-            high = v.astype(BF16).astype(F32)
-            vq[x * 9 + y] = jnp.where(low8, high, v - high)
+        ys = pl.ds(H, CY + 1)
+        v = w_s[H + x, ys]
+        for i in range(4):
+            v = v + y2[i] * pk[i, H + x, ys]
+        w_s[H + x, ys] = v
+        high = v.astype(BF16).astype(F32)
+        vq[x * 9:x * 9 + 9] = jnp.where(low8, high, v - high)
         return 0
 
-    lax.fori_loop(0, CX + 1, finish, 0)
+    for x in range(CX + 1):
+        finish(x, 0)
     for f in range(3):
         for x in range(CX):
             for y in range(CY):
@@ -553,8 +531,8 @@
 
     ci, cj, ck = cells(13)
     for c in range(2):
-        kt[:, c * 128:(c + 1) * 128] = jnp.where(zrow == ck + c, 1.0, 0.0).astype(BF16)
-    qg[...] = jnp.dot(vq[...].reshape(81 * 8, LANES).astype(BF16), kt[:, 0:256],
+        kt0[:, c * 128:(c + 1) * 128] = jnp.where(zrow == ck + c, 1.0, 0.0).astype(BF16)
+    qg[...] = jnp.dot(vq[...].reshape(81 * 8, LANES).astype(BF16), kt0[:, 0:256],
                       preferred_element_type=F32).reshape(81, 8, LANES)
     ci = jnp.broadcast_to(jnp.concatenate([ci, ci], axis=1), (8, LANES))
     cj = jnp.broadcast_to(jnp.concatenate([cj, cj], axis=1), (8, LANES))
@@ -610,6 +588,8 @@
             pltpu.VMEM((8, PTS, NB), F32),
             pltpu.VMEM((27, 48, NB), F32),
             pltpu.VMEM((LANES, 768), BF16),
+            pltpu.VMEM((LANES, 768), BF16),
+            pltpu.VMEM((81, 16, 768), BF16),
             pltpu.VMEM((81, 16, 768), BF16),
             ext, ext, ext, ext, ext, ext, ext, ext, ext, ext, ext,
             pltpu.VMEM((4, EX, EX, 8, LANES), F32),
@@ -618,8 +598,8 @@
             pltpu.VMEM((CX, 4, CZ), F32),
             pltpu.VMEM((9, CX, CY, 4, CZ), F32),
             pltpu.VMEM((9, 2, CX, 4, CZ), F32),
-            pltpu.VMEM((3, 3, 8, 128), F32),
-            pltpu.VMEM((3, 3, 7, 8, 128), F32),
+            pltpu.VMEM((3, 3, 16, 128), F32),
+            pltpu.VMEM((3, 3, 7, 16, 128), F32),
             pltpu.VMEM((3, PTS, NB), F32),
             pltpu.VMEM((81, 8, LANES), F32),
             pltpu.VMEM((81, 8, LANES), F32),

time: 105 us -> 85.2 us (0.81)
  Pallas kernels: 102 us -> 82.1 us
    pallas_call x1, Pallas kernels: 102 us -> 82.1 us  [shards(): pl.pallas_call(kernel, out_shape=(jax.ShapeDtypeStruct((3, CX, CY, CZ), F...]
where the time goes in v2:
time: 85.2 us; the launch traced here: 85 us
  Pallas kernels  82.1 us (96%)
  local copies, waits for them, and re-layouts  2.26 us (3%)
    pallas_call x1, Pallas kernels, shards(): pl.pallas_call(kernel, out_shape=(jax.ShapeDtypeStruct((3, CX, CY, CZ), F...  82.1 us
    unnamed x4, local copies, waits for them, and re-layouts  2.26 us

profile of v2, /device:TPU:2, one launch (start us, length us, event | category | flops | bytes accessed | tf_op | source)
XLA Modules:
  0.0 85.0 jit_solution(1008955408158028747)
XLA Ops:
  0.6 82.1 %granular_step.1 = (f32[3,8,8,128]{3,2,1,0:T(8,128)}, f32[3,128,128]{2,1,0:T(8,128)}) custom-call(f32[3,128,128]{2,1,0:T(8,128)} %bitcast.10, f32[128,128]{1,0:T(8,128)} %bitcast.12, f32[3,128,128]{2,1,0:T(8,128)} %bitcast.11, f32[128,128]{1,0:T(8,128)} %bitcast.13, s32[1,128]{1,0:T(1,128)} %bitcast.14, s32[1,128]{1,0:T(1,128)} %bitcast.15), custom_call_target="tpu_custom_call" | custom-call | tf_op jit(solution)/shard_map/granular_step/pallas_call | solution.py:582
  82.7 0.0 copy-start
  82.8 1.6 %copy.11 = f32[3,8,8,128]{3,2,1,0:T(8,128)} copy(f32[3,8,8,128]{3,2,1,0:T(8,128)} %get-tuple-element.10) | data formatting | bytes 196608
  84.3 0.0 copy-done
  84.3 0.7 copy.12
Async XLA Ops:
  82.7 1.6 %copy-start = (f32[3,128,128]{2,1,0:T(8,128)S(1)}, f32[3,128,128]{2,1,0:T(8,128)}, u32[]{:S(2)}) copy-start(f32[3,128,128]{2,1,0:T(8,128)} %get-tuple-element.5) | copy-start | bytes 589828

commit v3 on v2

--- a/solution.py
+++ b/solution.py
@@ -23,6 +23,7 @@
 BF16 = jnp.bfloat16
 C_ALL = 0.25 * (6.0 + 12.0 / 2.0 + 8.0 / 3.0)
 SHIFTS = (0.0, 0.85, 0.45, 0.2)
+SCALE = 2.0 ** 15
 PEERS = (4, 3, 5, 2, 6, 1, 7)
 PAIRS = [(i, j) for i in range(4) for j in range(i, 5)]
 NEAR = [o for o in itertools.product((-1, 0, 1), repeat=3) if any(o)]
@@ -80,7 +81,7 @@
     return quick_sum(q, r[0] / b[0])
 
 
-def coefficients(gram, hi):
+def coefficients(gram, theta, tau):
     zero = jnp.zeros_like(gram[0][0])
     g = {}
     for e, (i, j) in enumerate(PAIRS):
@@ -99,8 +100,6 @@
                 m = pair_mul(l[j, i], g[j, k])
                 g[i, k] = pair_add(g[i, k], (-m[0], -m[1]))
     low = {key: val[0] for key, val in l.items()}
-    theta = [hi * s for s in SHIFTS]
-    tau = [jnp.ones_like(hi)] + [hi * 0.5] * 3
     a = [theta[0] + tau[0] * low[0, 1]]
     for j in (1, 2, 3):
         a.append(theta[j] + (tau[j] * low[j, j + 1] - tau[j - 1] * low[j - 1, j]))
@@ -108,7 +107,7 @@
     c = [jnp.maximum(a[0], 1.0)]
     for j in (1, 2, 3):
         c.append(jnp.maximum(a[j] - tau[j - 1] * tau[j - 1] * ratio[j] / c[j - 1], 1.0))
-    f = [jnp.ones_like(hi)]
+    f = [jnp.ones_like(zero)]
     for j in (1, 2, 3):
         f.append(-(tau[j - 1] * f[j - 1]) / c[j - 1])
     z = [None] * 4
@@ -125,7 +124,7 @@
 
 def kernel(off, mass, vel, stiff, cell, live, v_out, u_out,
            tr, rx, kt0, kt1, am0, am1, dep, w_s, v0_s, a1_s, a2_s, mb_s, d_s, e_s, f_s, gs, ns, pk, p4,
-           v4, zp, rv, rz, ars, arb, ut, vq, qg,
+           v4, zp, rv, rz, ars, arb, vq, qg,
            dep_ss, dep_rs, v_ss, v_rs, ar_ss, ar_rs):
     me = [lax.axis_index(a) for a in AXES]
     kts, ams = (kt0, kt1), (am0, am1)
@@ -133,6 +132,7 @@
     def peer(o):
         return tuple(m if q == 0 else lax.rem(m + (q % N), N) for m, q in zip(me, o))
 
+    rx[:, 40:48, :] = jnp.zeros((27, 8, NB), F32)
     greeted = set((o[0] % N, o[1] % N, o[2] % N) for o in NEAR)
     for axis in range(3):
         for q in PEERS:
@@ -174,7 +174,6 @@
     for e in range(40):
         rx[13, e:e + 1, :] = jnp.sum(acc[e], axis=0, keepdims=True)
     rx[13, 40:41, :] = cell[...].astype(F32)
-    rx[13, 41:48, :] = jnp.zeros((7, NB), F32)
 
     pl.semaphore_wait(barrier, len(greeted))
 
@@ -183,7 +182,7 @@
 
     def deposit_copy(o):
         return pltpu.make_async_remote_copy(
-            src_ref=rx.at[13], dst_ref=rx.at[slot(neg(o))], send_sem=dep_ss.at[slot(o)],
+            src_ref=rx.at[13, pl.ds(0, 41)], dst_ref=rx.at[slot(neg(o)), pl.ds(0, 41)], send_sem=dep_ss.at[slot(o)],
             recv_sem=dep_rs.at[slot(neg(o))], device_id=peer(o), device_id_type=MESH)
 
     def v_copy(o):
@@ -268,39 +267,17 @@
         dup = jnp.where(low8, t, pltpu.roll(t, 4, 1))
         return jnp.where(empty, 0.0, dup / mb), mb, sb
 
-    def estimate(x, best):
-        v, mb, sb = node(x, pl.ds(H, CY + 1))
-        vv = v * v
-        damped = v * (1.0 + 0.6 * vv) / (1.0 + 0.9 * vv)
-        vv = jnp.where(low8, vv, damped * damped)
-        return jnp.maximum(best, jnp.max(mb * (1.0 + 0.9 * vv) + 5.0 * sb, axis=0))
-
-    best = lax.fori_loop(H, H + CX + 1, estimate, jnp.zeros((8, LANES), F32))
-    best = jnp.maximum(best[:, 0:128], best[:, 128:256])
-    ar_start(0, 0, (best, best))
-
     def wait_group(dx, dy):
         for dz in (-1, 0, 1):
             if (dx, dy, dz) != (0, 0, 0):
                 deposit_copy((-dx, -dy, -dz)).wait_recv()
 
-    def ar_max(k, p, best):
-        ar_wait(k, p)
-        for j in range(7):
-            best = jnp.maximum(best, arb[k, p, j, 0:8])
-        return best
-
-    best = ar_max(0, 0, best)
-    ar_start(0, 1, (best, best))
     wait_group(0, 0)
     add_group(0, 0, (-1, 1), 0)
     groups = [(-1, 0), (1, 0), (0, -1), (0, 1), (-1, -1), (-1, 1), (1, -1), (1, 1)]
     for i, (dx, dy) in enumerate(groups):
         wait_group(dx, dy)
         add_group(dx, dy, (-1, 0, 1), (i + 1) % 2)
-        if i == 4:
-            best = ar_max(0, 1, best)
-            ar_start(0, 2, (best, best))
 
     def coefs(x, _):
         v, mb, sb = node(x, pl.ds(0, EX))
@@ -313,7 +290,8 @@
         f_s[x] = jnp.where(row == 3, 0.125 * sb, a2 * v)
         return 0
 
-    lax.fori_loop(0, EX, coefs, 0)
+    for x in range(EX):
+        coefs(x, 0)
 
     def level(k, emit):
         first, last = H - k, H + CX + k
@@ -345,6 +323,12 @@
         mvv = mb * v * v
         e_s[x, ys] = mb + 0.9 * mvv + d
         p = jnp.where(empty, 0.0, lq - (d + 0.3 * mvv) * v)
+        if H <= x < H + CX:
+            own = slice(4, 4 + CY)
+            vo, mo, do = v[own, :, 0:CZ], mb[own, :, 0:CZ], d[own, :, 0:CZ]
+            vv = vo * vo
+            damped = vo * (1.0 + 0.6 * vv) / (1.0 + 0.9 * vv)
+            largest.append(jnp.max(mo * (1.0 + 0.9 * damped * damped) + do, axis=0))
         pk[0, x, ys] = p
         f_s[x, ys] = a2_s[x, ys] * p
 
@@ -359,20 +343,19 @@
         pk[0, x, ys] = p
         f_s[x, ys] = a2_s[x, ys] * p
 
-    def basis(k, hi):
+    def basis(k, shift, factor):
         lanes = CZ if k == 3 else LANES
         wide = pl.ds(0, lanes)
-        theta = jnp.broadcast_to(hi * SHIFTS[k], (8, lanes))
-        inv = jnp.broadcast_to(2.0 / hi, (8, lanes))
+        if shift is not None:
+            shift = jnp.broadcast_to(shift, (8, lanes))
+        factor = jnp.broadcast_to(factor, (8, lanes))
 
         def emit(x, ys, sums):
             lq = folded(x, ys, sums, wide)
             e = e_s[x, ys, :, wide]
-            if k:
-                e = e - theta
-            p = e * pk[k, x, ys, :, wide] - lq
-            if k:
-                p = p * inv
+            if shift is not None:
+                e = e - shift
+            p = (e * pk[k, x, ys, :, wide] - lq) * factor
             if k == 3:
                 p4[x - H] = p
             else:
@@ -416,15 +399,21 @@
             packed.append(a)
         return tuple(jnp.where(lane < 64, packed[0][i], packed[1][i]) for i in range(2))
 
+    extra = (rows8 == 7) & (lane >= 64)
+
     def ar_sum(k, p, own):
         ar_wait(k, p)
         terms = [own] + [(arb[k, p, j, 0:8], arb[k, p, j, 8:16]) for j in range(7)]
         while len(terms) > 1:
             terms = [pair_add(terms[i], terms[i + 1]) for i in range(0, len(terms), 2)]
-        return terms[0]
-
-    def solve(k, hi, idle):
-        g = gram()
+        if k:
+            return terms[0]
+        best = own[0]
+        for j in range(7):
+            best = jnp.maximum(best, arb[k, p, j, 0:8])
+        return jnp.where(extra, best, terms[0][0]), jnp.where(extra, 0.0, terms[0][1])
+
+    def solve(k, g, idle):
         for p in range(3):
             ar_start(k, p, g)
             if p == 0:
@@ -434,15 +423,13 @@
         for e in range(14):
             r, base = e % 8, 64 * (e // 8)
             entries.append(tuple(jnp.broadcast_to(q[r:r + 1, base:base + 1], (8, 128)) for q in g))
-        return coefficients(entries, hi)
-
+        return entries, g
+
+    largest = []
     level(4, first_residual)
-    basis(0, jnp.ones((1, 1), F32))
-    best = ar_max(0, 2, best)
-    hi1 = jnp.max(jnp.max(jnp.where(low, best, 0.0), axis=0, keepdims=True), axis=1, keepdims=True)
-    hi2 = jnp.max(jnp.max(jnp.where(low, 0.0, best), axis=0, keepdims=True), axis=1, keepdims=True)
-    for k in (1, 2, 3):
-        basis(k, hi1)
+    for k in range(4):
+        basis(k, None, jnp.full((1, 1), 1.0 / SCALE, F32))
+
     def keep_target():
         def plane(x, _):
             v0_s[x] = w_s[x]
@@ -450,7 +437,14 @@
 
         lax.fori_loop(1, EX - 1, plane, 0)
 
-    y1 = solve(1, jnp.broadcast_to(hi1, (8, 128)), keep_target)
+    best = functools.reduce(jnp.maximum, largest)
+    best = jnp.max(jnp.max(best, axis=0, keepdims=True), axis=1, keepdims=True)
+    g = gram()
+    g = (jnp.where(extra, jnp.broadcast_to(best, (8, 128)), g[0]), g[1])
+    entries, g = solve(0, g, keep_target)
+    hi2 = g[0][7:8, 64:65]
+    same = [jnp.full((8, 128), SCALE, F32)] * 4
+    y1 = coefficients(entries, [0.0] * 4, same)
 
     slots = [(lane >= 16 * y - 5) & (lane < 16 * y + 5) for y in range(8)]
     slots[0] = (lane < 5) | (lane >= 123)
@@ -508,8 +502,10 @@
 
     level(4, second_residual)
     for k in range(4):
-        basis(k, hi2)
-    y2 = solve(2, jnp.broadcast_to(hi2, (8, 128)), lambda: None)
+        basis(k, hi2 * SHIFTS[k] if k else None, 2.0 / hi2 if k else jnp.ones((1, 1), F32))
+    entries, _ = solve(1, gram(), lambda: None)
+    hi2 = jnp.broadcast_to(hi2, (8, 128))
+    y2 = coefficients(entries, [hi2 * s for s in SHIFTS], [jnp.ones((8, 128), F32)] + [hi2 * 0.5] * 3)
     y2 = [jnp.concatenate([q, q], axis=1) for q in y2]
 
     def finish(x, _):
@@ -561,17 +557,14 @@
                 r = corner[key]
                 term = wt * (gz * r[f:f + 1, 0:128] + fz * r[f:f + 1, 128:256])
                 total = term if total is None else total + term
-            ut[f, at] = total
+            u_out[f, at] = total
         return 0
 
     lax.fori_loop(0, PTS // 8, points, 0)
-    for f in range(3):
-        u_out[f] = ut[f].T
-
     for o in order:
         deposit_copy(o).wait_send()
         v_copy(o).wait_send()
-    for k in range(3):
+    for k in range(2):
         for p in range(3):
             pltpu.make_async_copy(arb.at[k, p], arb.at[k, p], ar_ss.at[k, p]).wait()
 
@@ -581,7 +574,7 @@
     ext = pltpu.VMEM((EX, EX, 8, LANES), F32)
     v, u = pl.pallas_call(
         kernel,
-        out_shape=(jax.ShapeDtypeStruct((3, CX, CY, CZ), F32), jax.ShapeDtypeStruct((3, NB, PTS), F32)),
+        out_shape=(jax.ShapeDtypeStruct((3, CX, CY, CZ), F32), jax.ShapeDtypeStruct((3, PTS, NB), F32)),
         in_specs=[vm] * 6,
         out_specs=(vm, vm),
         scratch_shapes=[
@@ -598,17 +591,16 @@
             pltpu.VMEM((CX, 4, CZ), F32),
             pltpu.VMEM((9, CX, CY, 4, CZ), F32),
             pltpu.VMEM((9, 2, CX, 4, CZ), F32),
-            pltpu.VMEM((3, 3, 16, 128), F32),
-            pltpu.VMEM((3, 3, 7, 16, 128), F32),
-            pltpu.VMEM((3, PTS, NB), F32),
+            pltpu.VMEM((2, 3, 16, 128), F32),
+            pltpu.VMEM((2, 3, 7, 16, 128), F32),
             pltpu.VMEM((81, 8, LANES), F32),
             pltpu.VMEM((81, 8, LANES), F32),
             pltpu.SemaphoreType.DMA((27,)),
             pltpu.SemaphoreType.DMA((27,)),
             pltpu.SemaphoreType.DMA((27,)),
             pltpu.SemaphoreType.DMA((27,)),
-            pltpu.SemaphoreType.DMA((3, 3)),
-            pltpu.SemaphoreType.DMA((3, 3)),
+            pltpu.SemaphoreType.DMA((2, 3)),
+            pltpu.SemaphoreType.DMA((2, 3)),
         ],
         compiler_params=pltpu.CompilerParams(
             collective_id=0, has_side_effects=True, vmem_limit_bytes=60 << 20),
@@ -621,7 +613,7 @@
         cell_index.reshape(1, NB),
         live_count.reshape(1, NB),
     )
-    return v, u.reshape(3, 1, 1, 1, NB, PTS)
+    return v, u.transpose(0, 2, 1).reshape(3, 1, 1, 1, NB, PTS)
 
 
 def solution(mesh):

time: 85.2 us -> 83.6 us (0.981)
  Pallas kernels: 82.1 us -> 80.4 us
    pallas_call x1, Pallas kernels: 82.1 us -> 80.4 us  [shards(): pl.pallas_call(kernel, out_shape=(jax.ShapeDtypeStruct((3, CX, CY, CZ), F...]
where the time goes in v3:
time: 83.6 us; the launch traced here: 83.4 us
  Pallas kernels  80.4 us (96%)
  local copies, waits for them, and re-layouts  2.42 us (3%)
    pallas_call x1, Pallas kernels, shards(): pl.pallas_call(kernel, out_shape=(jax.ShapeDtypeStruct((3, CX, CY, CZ), F...  80.4 us
    unnamed x4, local copies, waits for them, and re-layouts  2.42 us

profile of v3, /device:TPU:2, one launch (start us, length us, event | category | flops | bytes accessed | tf_op | source)
XLA Modules:
  0.0 83.4 jit_solution(9971666833600553676)
XLA Ops:
  0.6 80.4 %granular_step.1 = (f32[3,8,8,128]{3,2,1,0:T(8,128)}, f32[3,128,128]{2,1,0:T(8,128)}) custom-call(f32[3,128,128]{2,1,0:T(8,128)} %bitcast.10, f32[128,128]{1,0:T(8,128)} %bitcast.12, f32[3,128,128]{2,1,0:T(8,128)} %bitcast.11, f32[128,128]{1,0:T(8,128)} %bitcast.13, s32[1,128]{1,0:T(1,128)} %bitcast.14, s32[1,128]{1,0:T(1,128)} %bitcast.15), custom_call_target="tpu_custom_call" | custom-call | tf_op jit(solution)/shard_map/granular_step/pallas_call | solution.py:575
  81.0 0.0 copy-start
  81.0 1.8 %copy.8 = f32[3,1,1,1,128,128]{5,4,3,2,1,0:T(8,128)} copy(f32[3,1,1,1,128,128]{4,5,0,3,2,1:T(8,128)} %bitcast.9) | data formatting | bytes 393216
  82.8 0.0 copy-done
  82.8 0.6 copy.10
Async XLA Ops:
  81.0 1.8 %copy-start = (f32[3,8,8,128]{3,2,1,0:T(8,128)S(1)}, f32[3,8,8,128]{3,2,1,0:T(8,128)}, u32[]{:S(2)}) copy-start(f32[3,8,8,128]{3,2,1,0:T(8,128)} %get-tuple-element.10) | copy-start | bytes 294916
